TPU v7x, 32 devices: a whole 2x2x4 slice. The times are simulated.
32 devices in a mesh: space: 16 (over z, y, x), rep: 2 (over core).
Axes of the slice: x: 2, y: 2, z: 4, core: 2. Of those that a mesh axis runs over, the one named last changes fastest.
Arguments:
- features: bfloat16 [2, 64, 64, 512], P('rep', 'space'), may hold values from -6 to 6
- neighbours: int32 [2, 64, 26], P('rep', 'space'), may hold values from -1 to 35, as said below
- send_list: int32 [2, 16, 2, 16], P('rep', 'space'), may hold values from -1 to 3, as said below
- w_fine: bfloat16 [64, 1728], replicated, may hold values from -0.15625 to 0.15625
- w_down: bfloat16 [64, 512], replicated, may hold values from -0.25 to 0.25
- w_coarse: bfloat16 [64, 1728], replicated, may hold values from -0.15625 to 0.15625
- w_up: bfloat16 [64, 512], replicated, may hold values from -0.75 to 0.75
- cotangent: bfloat16 [2, 64, 64, 512], P('rep', 'space'), may hold values from -6 to 6
Outputs:
- decoded: bfloat16 [2, 64, 64, 512], P('rep', 'space')
- grad_fine: float32 [64, 1728], replicated
- grad_down: float32 [64, 512], replicated
- grad_coarse: float32 [64, 1728], replicated
- grad_up: float32 [64, 512], replicated
Inputs may be any that keep to these rules, and one draw needn't show every extreme that they name: `neighbours`: A scene is a corridor 4 block positions across in the second and third dimensions; device d holds the occupied positions whose first coordinate lies in 4 d .. 4 d + 3, in Morton order. Entries follow true adjacency: below 4 a block of the same device, 4 + s (s < 4**2) the block of device d - 1 in slot s of its side 0, 4 + 4**2 + s the block of device d + 1 in slot s of its side 1, -1 an empty or outside position. In every slab the positions (0, 3, 3) and (3, 3, 3) are occupied and (3, 0, 0) is empty. send_list[d, 0, y * 4 + z] is device d's block at the last first-coordinate plane of its slab and position (y, z), send_list[d, 1, y * 4 + z] the one at the first plane; -1 where that position is empty.
All inputs are finite; a program needn't handle non-finite values.
Results may differ from a plain program's by a relative error of at most 0.007.
Values may be sent and summed in bfloat16 or wider, within the bound.
A program may use at most 128 MiB of HBM per device.

v0:
```python
import functools
import math

import jax
import jax.numpy as jnp
import numpy as np
from jax import lax
from jax.experimental import pallas as pl
from jax.experimental.pallas import tpu as pltpu
from jax.sharding import PartitionSpec as P

EDGE = 8
HALF = EDGE // 2
TILE = 128
F32 = jnp.float32
BF16 = jnp.bfloat16
MESH = pl.DeviceIdType.MESH


def spots(step, side):
    if step < 0:
        return [(side - 1, 0)]
    if step == 0:
        return [(v, v + 1) for v in range(side)]
    return [(0, side + 1)]


def fine_spread():
    table = np.zeros((9, 2, EDGE, EDGE, 2, TILE), np.float32)
    for j in (-1, 0, 1):
        for l in (-1, 0, 1):
            for y, py in spots(j, EDGE):
                for z, pz in spots(l, EDGE):
                    for x in range(2):
                        table[3 * (j + 1) + l + 1, x, y, z, x, (EDGE + 2) * py + pz] = 1
    return table.reshape(9 * 2 * EDGE * EDGE, 2 * TILE)


def coarse_spread():
    table = np.zeros((10, HALF, HALF, HALF, HALF, TILE), np.float32)
    for j in (-1, 0, 1):
        for l in (-1, 0, 1):
            for y, py in spots(j, HALF):
                for z, pz in spots(l, HALF):
                    for x in range(HALF):
                        table[3 * (j + 1) + l + 1, x, y, z, x, (HALF + 2) * py + pz] = 1
    return table.reshape(10 * HALF**3, HALF * TILE)


def pair_spread():
    centre = coarse_spread().reshape(10, HALF**3, HALF, TILE)[4]
    return np.concatenate([centre, np.roll(centre, 64, axis=-1)]).reshape(2 * HALF**3, HALF * TILE)


def patch_order():
    table = np.zeros((EDGE**3, EDGE**3), np.float32)
    for x in range(EDGE):
        for y in range(EDGE):
            for z in range(EDGE):
                part = 4 * (x % 2) + 2 * (y % 2) + z % 2
                cell = (x // 2 * HALF + y // 2) * HALF + z // 2
                table[(x * EDGE + y) * EDGE + z, part * HALF**3 + cell] = 1
    return table


def dot(a, b):
    return jnp.dot(a, b, preferred_element_type=F32)


def dot_t(a, b):
    return lax.dot_general(a, b, (((1,), (1,)), ((), ())), preferred_element_type=F32)


def split_dot(f, a, b):
    high = a.astype(BF16)
    low = (a - high.astype(F32)).astype(BF16)
    return f(high, b) + f(low, b)


def tiles(x):
    return [x[:, TILE * t : TILE * (t + 1)] for t in range(x.shape[1] // TILE)]


def turn(x, shift):
    shift = shift % TILE
    if shift == 0:
        return x
    return jnp.concatenate([pltpu.roll(t, shift, axis=1) for t in tiles(x)], axis=1)


def sigmoid(v):
    return 1.0 / (1.0 + jnp.exp(-v))


def placed(x, tile_count):
    rows = []
    for a in range(3):
        parts = []
        if a:
            parts.append(jnp.zeros((x.shape[0], a * TILE), x.dtype))
        parts.append(x)
        if a < 2:
            parts.append(jnp.zeros((x.shape[0], (2 - a) * TILE), x.dtype))
        rows.append(jnp.concatenate(parts, axis=1))
    return jnp.concatenate(rows, axis=0)


def body(
    peers,
    f_ref, nb_ref, sl_ref, cot_ref, wf_ref, wd_ref, wc_ref, wct_ref, wu_ref, wdt_ref, wut_ref,
    e0_ref, q0_ref, q2_ref, pm_ref,
    out_ref, grads_ref,
    x0, fh, fl, sl_lo, sl_hi, sm_lo, sm_hi, idx, r0, slope0, p2, c2, h1, h1_lo, h1_hi,
    cand, r1, rim, rim_lo, rim_hi, dg0, dgm, dgp, gh1, gh0,
    send_sem, recv_sem, local_sem,
):
    nb, ch = f_ref.shape[0], f_ref.shape[1]
    cells = HALF**3
    me = lax.axis_index("space")
    rep = lax.axis_index("rep")
    up = lax.rem(me + 1, peers)
    down = lax.rem(me + peers - 1, peers)

    barrier = pltpu.get_barrier_semaphore()
    for other in (up, down):
        pl.semaphore_signal(barrier, inc=1, device_id=(other, rep), device_id_type=MESH)
    pl.semaphore_wait(barrier, 2)

    def remote(src, dst, n, other):
        copy = pltpu.make_async_remote_copy(
            src_ref=src, dst_ref=dst, send_sem=send_sem.at[n], recv_sem=recv_sem.at[n],
            device_id=(other, rep), device_id_type=MESH,
        )
        copy.start()
        return copy

    last = f_ref.shape[2] - TILE
    first = [
        remote(sl_ref, sl_lo, 0, up),
        remote(sl_ref, sl_hi, 1, down),
        remote(f_ref.at[:, :, last:], fh.at[nb : 2 * nb], 2, up),
        remote(f_ref.at[:, :, :TILE], fl.at[nb : 2 * nb], 3, down),
    ]

    x0[:nb] = f_ref[...]
    x0[nb] = jnp.zeros(x0.shape[1:], BF16)
    fh[:nb] = f_ref[:, :, last:]
    fl[:nb] = f_ref[:, :, :TILE]
    fh[2 * nb] = jnp.zeros(fh.shape[1:], BF16)
    fl[2 * nb] = jnp.zeros(fl.shape[1:], BF16)

    def to_patches(src, dst, b):
        moved = dot(src, pm_ref[...]).astype(BF16)
        for part in range(8):
            dst[part * ch : (part + 1) * ch, b * cells : (b + 1) * cells] = moved[
                :, part * cells : (part + 1) * cells
            ]

    for b in range(nb):
        to_patches(cot_ref[b], c2, b)

    first[0].wait()
    first[1].wait()
    to_smem = [
        pltpu.make_async_copy(sl_lo, sm_lo, local_sem.at[0]),
        pltpu.make_async_copy(sl_hi, sm_hi, local_sem.at[1]),
    ]
    for copy in to_smem:
        copy.start()
    for copy in to_smem:
        copy.wait()
    slots = sl_ref.shape[1]
    none = 2 * nb
    for b in range(nb):
        for k in range(27):
            if k == 13:
                idx[b, k] = jnp.int32(b)
                continue
            v = nb_ref[b, k if k < 13 else k - 1]
            if k < 9:
                far = nb + sm_lo[0, jnp.clip(v - nb, 0, slots - 1)]
                v = jnp.where(v < 0, none, jnp.where(v < nb, v, far))
            elif k >= 18:
                far = nb + sm_hi[1, jnp.clip(v - nb - slots, 0, slots - 1)]
                v = jnp.where(v < 0, none, jnp.where(v < nb, v, far))
            else:
                v = jnp.where(v < 0, nb, v)
            idx[b, k] = v
    first[2].wait()
    first[3].wait()

    e0 = e0_ref[...]
    e0c = e0_ref[4 * TILE : 5 * TILE, :]
    for b in range(nb):
        rows = []
        for t in range(4):
            rows.append(
                jnp.concatenate(
                    [x0[idx[b, 9 + n], :, t * TILE : (t + 1) * TILE] for n in range(9)], axis=1
                )
            )
        inner = dot(jnp.concatenate(rows, axis=0), e0)
        low = dot(jnp.concatenate([fh[idx[b, n]] for n in range(9)], axis=1), e0[:, TILE:])
        high = dot(jnp.concatenate([fl[idx[b, 18 + n]] for n in range(9)], axis=1), e0[:, :TILE])
        pad = jnp.concatenate(
            [low] + [inner[t * ch : (t + 1) * ch] for t in range(4)] + [high], axis=1
        )
        for n in range(9):
            off = (EDGE + 2) * (n // 3 - 1) + n % 3 - 1
            r0[b, n * ch : (n + 1) * ch, :] = turn(pad, -off).astype(BF16)
        y = dot(wf_ref[...], r0[b])
        wide = EDGE * TILE
        v = sum(y[a * ch : (a + 1) * ch, a * TILE : a * TILE + wide] for a in range(3))
        s = sigmoid(v)
        slope0[b] = s * (1.0 + v * (1.0 - s))
        h = (v * s).astype(BF16)
        flat = jnp.concatenate(
            [dot_t(h[:, 2 * TILE * t : 2 * TILE * (t + 1)], e0c).astype(BF16) for t in range(4)],
            axis=1,
        )
        to_patches(flat, p2, b)

    coarse_pre = dot(wd_ref[...], p2[...])
    s = sigmoid(coarse_pre)
    slope_down = s * (1.0 + coarse_pre * (1.0 - s))
    hidden1 = (coarse_pre * s).astype(BF16)
    h1[...] = hidden1
    second = [remote(h1, h1_lo, 4, up), remote(h1, h1_hi, 5, down)]

    lane = lax.broadcasted_iota(jnp.int32, (ch, TILE), 1)
    left = lane < cells
    nothing = jnp.zeros((ch, TILE), F32)

    def candidates(value, table, base):
        for b in range(nb):
            x = value[:, (b // 2) * TILE : (b // 2 + 1) * TILE].astype(F32)
            swapped = pltpu.roll(x, cells, axis=1)
            on_left, on_right = (x, swapped) if b % 2 == 0 else (swapped, x)
            cand[table, 0, base + b] = jnp.where(left, on_left, nothing).astype(BF16)
            cand[table, 1, base + b] = jnp.where(left, nothing, on_right).astype(BF16)

    for table in range(3):
        candidates(hidden1, table, 0)
        for half in range(2):
            cand[table, half, none] = nothing.astype(BF16)
            if table == 1:
                for n in range(nb, 2 * nb):
                    cand[table, half, n] = nothing.astype(BF16)
    up_back = dot(wu_ref[...], c2[...])
    for copy in second:
        copy.wait()
    candidates(h1_lo[...], 0, nb)
    candidates(h1_hi[...], 2, nb)

    q0 = q0_ref[...]
    top = (HALF - 1) * TILE

    def sources(b, i):
        parts = []
        for t in range(5):
            x = cand[i, 0, idx[b, 9 * i + 2 * t]]
            if t < 4:
                x = x + cand[i, 1, idx[b, 9 * i + 2 * t + 1]]
            parts.append(x)
        return jnp.concatenate(parts, axis=1)

    pairs = nb // 2
    wide1 = HALF * TILE
    gated = []
    delta_up = []
    for p in range(pairs):
        pads = []
        for b in (2 * p, 2 * p + 1):
            pads.append(
                jnp.concatenate(
                    [
                        dot(sources(b, 0), q0[:, top:]),
                        dot(sources(b, 1), q0),
                        dot(sources(b, 2), q0[:, :TILE]),
                    ],
                    axis=1,
                )
            )
        pad = pads[0] + turn(pads[1], cells)
        for n in range(9):
            off = (HALF + 2) * (n // 3 - 1) + n % 3 - 1
            r1[p, n * ch : (n + 1) * ch, :] = turn(pad, -off).astype(BF16)
        y = dot(wc_ref[...], r1[p])
        v = sum(y[a * ch : (a + 1) * ch, a * TILE : a * TILE + wide1] for a in range(3))
        s = sigmoid(v)
        slope = s * (1.0 + v * (1.0 - s))
        gated.append(dot_t((v * s).astype(BF16), q2_ref[...]).astype(BF16))
        ub = split_dot(dot, up_back[:, p * TILE : (p + 1) * TILE], q2_ref[...])
        delta = (ub * slope).astype(BF16)
        delta_up.append(delta)
        turned = []
        for n in range(9):
            off = (HALF + 2) * (n // 3 - 1) + n % 3 - 1
            turned.append(turn(delta.astype(F32), off).astype(BF16))
        y = dot(wct_ref[...], jnp.concatenate(turned, axis=0))
        gap = jnp.zeros((ch, TILE), F32)
        back = (
            jnp.concatenate([y[:ch], gap, gap], axis=1)
            + jnp.concatenate([gap, y[ch : 2 * ch], gap], axis=1)
            + jnp.concatenate([gap, gap, y[2 * ch :]], axis=1)
        )
        rim[0, p] = back[:, :TILE].astype(BF16)
        rim[1, p] = back[:, -TILE:].astype(BF16)
        for h in range(2):
            b = 2 * p + h
            x = turn(back, -h * cells)
            dg0[b] = split_dot(dot_t, x[:, TILE : TILE + wide1], q0)
            dgm[b] = split_dot(dot_t, x[:, :TILE], q0[:, top:])
            dgp[b] = split_dot(dot_t, x[:, -TILE:], q0[:, :TILE])
    third = [remote(rim.at[0], rim_hi, 6, down), remote(rim.at[1], rim_lo, 7, up)]

    gated = jnp.concatenate(gated, axis=1)
    dec = (p2[...].astype(F32) + dot(wut_ref[...], gated)).astype(BF16)

    def from_patches(value, b):
        return jnp.concatenate(
            [value[n * ch : (n + 1) * ch, b * cells : (b + 1) * cells] for n in range(8)], axis=1
        )

    for b in range(nb):
        out_ref[b] = dot_t(from_patches(dec, b), pm_ref[...]).astype(BF16)
    taps = 9 * ch
    grad_coarse = sum(dot_t(placed(delta_up[p], HALF), r1[p]) for p in range(pairs))
    for a in range(3):
        grads_ref[:, (3 + a) * taps : (4 + a) * taps] = grad_coarse[a * ch : (a + 1) * ch]
    grads_ref[:, 6 * taps + 8 * ch : 6 * taps + 16 * ch] = dot_t(gated, c2[...])

    dg0[nb] = jnp.zeros(dg0.shape[1:], F32)
    dgm[none] = jnp.zeros(dg0.shape[1:], F32)
    dgp[none] = jnp.zeros(dg0.shape[1:], F32)
    for copy in third:
        copy.wait()
    for p in range(pairs):
        for h in range(2):
            x = turn(rim_hi[p].astype(F32), -h * cells).astype(BF16)
            dgm[nb + 2 * p + h] = dot_t(x, q0[:, top:])
            x = turn(rim_lo[p].astype(F32), -h * cells).astype(BF16)
            dgp[nb + 2 * p + h] = dot_t(x, q0[:, :TILE])
    for b in range(nb):
        sums = [nothing, nothing]
        for k in range(27):
            chunk = 8 - k % 9
            table = (dgp, dg0, dgm)[k // 9]
            t = chunk // 2
            sums[chunk % 2] = sums[chunk % 2] + table[idx[b, k], :, t * TILE : (t + 1) * TILE]
        gh1[:, b * cells : (b + 1) * cells] = sums[0][:, :cells] + sums[1][:, cells:]
    delta_down = (gh1[...] * slope_down).astype(BF16)
    grads_ref[:, 6 * taps : 6 * taps + 8 * ch] = dot_t(delta_down, p2[...])
    gh0[...] = c2[...].astype(F32) + dot(wdt_ref[...], delta_down)
    grad_fine = jnp.zeros((3 * ch, taps), F32)
    for b in range(nb):
        flat = dot_t(from_patches(gh0[...], b).astype(BF16), pm_ref[...]).astype(BF16)
        wide_grad = jnp.concatenate([dot(t, e0c) for t in tiles(flat)], axis=1)
        delta = (wide_grad * slope0[b]).astype(BF16)
        grad_fine = grad_fine + dot_t(placed(delta, EDGE), r0[b])
    for a in range(3):
        grads_ref[:, a * taps : (a + 1) * taps] = grad_fine[a * ch : (a + 1) * ch]


def shards(features, neighbours, send_list, w_fine, w_down, w_coarse, w_up, cotangent):
    nb, ch = features.shape[1], features.shape[2]
    cols = nb * HALF**3
    peers = lax.axis_size("space")
    taps = 9 * ch

    def stacked(w):
        return w.reshape(ch, 3, taps).transpose(1, 0, 2).reshape(3 * ch, taps)

    wct = w_coarse.reshape(ch, 3, 9, ch).transpose(1, 3, 2, 0).reshape(3 * ch, taps)
    consts = [jnp.asarray(t(), BF16) for t in (fine_spread, coarse_spread, pair_spread, patch_order)]
    vmem = pl.BlockSpec(memory_space=pltpu.VMEM)
    smem = pl.BlockSpec(memory_space=pltpu.SMEM)
    v = pltpu.VMEM
    width = 10 * HALF**3
    decoded, grads = pl.pallas_call(
        functools.partial(body, peers),
        out_shape=(
            jax.ShapeDtypeStruct(features.shape[1:], BF16),
            jax.ShapeDtypeStruct((ch, 6 * taps + 16 * ch), F32),
        ),
        in_specs=[vmem, smem] + [vmem] * 13,
        out_specs=(vmem, vmem),
        scratch_shapes=[
            v((nb + 1, ch, EDGE**3), BF16),
            v((2 * nb + 1, ch, TILE), BF16),
            v((2 * nb + 1, ch, TILE), BF16),
            v(send_list.shape[2:], jnp.int32),
            v(send_list.shape[2:], jnp.int32),
            pltpu.SMEM(send_list.shape[2:], jnp.int32),
            pltpu.SMEM(send_list.shape[2:], jnp.int32),
            pltpu.SMEM((nb, 27), jnp.int32),
            v((nb, taps, (EDGE + 2) * TILE), BF16),
            v((nb, ch, EDGE * TILE), F32),
            v((8 * ch, cols), BF16),
            v((8 * ch, cols), BF16),
            v((ch, cols), BF16),
            v((ch, cols), BF16),
            v((ch, cols), BF16),
            v((3, 2, 2 * nb + 1, ch, TILE), BF16),
            v((nb // 2, taps, (HALF + 2) * TILE), BF16),
            v((2, nb // 2, ch, TILE), BF16),
            v((nb // 2, ch, TILE), BF16),
            v((nb // 2, ch, TILE), BF16),
            v((nb + 1, ch, width), F32),
            v((2 * nb + 1, ch, width), F32),
            v((2 * nb + 1, ch, width), F32),
            v((ch, cols), F32),
            v((8 * ch, cols), F32),
            pltpu.SemaphoreType.DMA((8,)),
            pltpu.SemaphoreType.DMA((8,)),
            pltpu.SemaphoreType.DMA((2,)),
        ],
        compiler_params=pltpu.CompilerParams(
            collective_id=0, has_side_effects=True, vmem_limit_bytes=56 * 1024 * 1024
        ),
    )(
        features[0], neighbours[0], send_list[0, 0], cotangent[0],
        stacked(w_fine), w_down, stacked(w_coarse), wct, w_up, w_down.T, w_up.T, *consts,
    )
    factor = 1.0 / math.sqrt(lax.axis_size("rep") * peers * nb * EDGE**3)
    grads = lax.psum(grads, ("space", "rep")) * factor
    a, b, c = 3 * taps, 6 * taps, 6 * taps + 8 * ch
    return decoded[None], grads[:, :a], grads[:, b:c], grads[:, a:b], grads[:, c:]


def solution(mesh):
    in_specs = (
        P("rep", "space", None, None),
        P("rep", "space", None),
        P("rep", "space", None, None),
        P(),
        P(),
        P(),
        P(),
        P("rep", "space", None, None),
    )
    out_specs = (P("rep", "space", None, None), P(), P(), P(), P())
    return jax.shard_map(shards, mesh=mesh, in_specs=in_specs, out_specs=out_specs, check_vma=False)
```

profile of v0, /device:TPU:0, one launch (start us, length us, event | category | flops | bytes accessed | tf_op | source)
XLA Modules:
  0.0 195.4 jit_solution(12918302727934356096)
XLA Ops:
  7.2 0.0 copy-start
  7.2 0.0 copy-start.1
  7.2 0.0 copy-start.3
  7.2 0.0 all-reduce.2.cloned.1.call-start
  7.2 1.2 reshape.30
  8.5 1.2 copy.24
  9.7 0.0 copy-done
  9.7 0.8 copy.26
  10.4 0.0 copy-done.1
  10.4 0.8 copy.27
  11.2 0.0 copy-done.3
  11.2 0.2 reshape.28
  11.4 0.7 copy.22
  12.1 0.7 copy.23
  12.8 0.3 copy.29
  13.2 1.1 reshape.34.wct_ref
  14.3 38.5 %shard_map.155 = (bf16[4,64,512]{2,1,0:T(8,128)(2,1)}, f32[64,4480]{1,0:T(8,128)}) custom-call(bf16[4,64,512]{2,1,0:T(8,128)(2,1)} %bitcast.21, s32[4,26]{1,0:T(4,128)} %bitcast.24, s32[2,16]{1,0:T(2,128)} %bitcast.25, bf16[4,64,512]{2,1,0:T(8,128)(2,1)} %bitcast.22, bf16[192,576]{1,0:T(8,128)(2,1)} %bitcast.17, bf16[64,512]{1,0:T(8,128)(2,1)} %wd_ref.1, ...), custom_call_target="tpu_custom_call" | custom-call | tf_op jit(solution)/shard_map/pallas_call | solution.py:380
  52.8 0.0 all-reduce.2.cloned.1.call-update
  52.8 131.9 %all-reduce.2.cloned.1.call-done = f32[64,4480]{1,0:T(8,128)} async-done(((f32[64,4480]{1,0:T(8,128)}), f32[64,4480]{1,0:T(8,128)}) %all-reduce.2.cloned.1.call-update) | async-done | bytes 1146896 | tf_op jit(solution)/shard_map/psum | solution.py:426
  184.7 1.3 broadcast_multiply_fusion
  186.0 0.0 copy-start.2
  186.0 0.7 fusion
  186.8 1.0 fusion.1
  187.8 0.0 copy-done.2
  187.8 0.7 copy.33
Async XLA Ops:
  7.2 2.5 %copy-start = (bf16[64,512]{1,0:T(8,128)(2,1)S(1)}, bf16[64,512]{1,0:T(8,128)(2,1)}, u32[]{:S(2)}) copy-start(bf16[64,512]{1,0:T(8,128)(2,1)} %wd_ref.1) | copy-start | bytes 196612
  7.2 3.3 %copy-start.1 = (bf16[64,512]{1,0:T(8,128)(2,1)S(1)}, bf16[64,512]{1,0:T(8,128)(2,1)}, u32[]{:S(2)}) copy-start(bf16[64,512]{1,0:T(8,128)(2,1)} %wu_ref.1) | copy-start | bytes 196612
  7.2 4.0 %copy-start.3 = (bf16[64,1728]{1,0:T(8,128)(2,1)S(1)}, bf16[64,1728]{1,0:T(8,128)(2,1)}, u32[]{:S(2)}) copy-start(bf16[64,1728]{1,0:T(8,128)(2,1)} %param.15) | copy-start | bytes 663556
  7.2 177.5 %all-reduce.2.cloned.1.call-start = ((), (), s32[]{:S(2)}) async-start(), calls=%async_computation | async-start | bytes 2293760 | tf_op jit(solution)/shard_map/psum | solution.py:426
  186.0 1.8 copy-start.2
Sparse Core Ops, SparseCore 0:
  52.9 131.7 all-reduce.1
where the time goes:
time: 196 us; the launch traced here: 195 us
  waiting for transfers between devices  132 us (67%)
  Pallas kernels  38.5 us (20%)
  between operations  14.1 us (7%)
  local copies, waits for them, and re-layouts  9.49 us (5%)
    psum x1, waiting for transfers between devices, shards(): grads = lax.psum(grads, ('space', 'rep')) * factor  132 us
    pallas_call x1, Pallas kernels, shards(): pl.pallas_call(functools.partial(body, peers), out_shape=(jax.ShapeDtypeS...  38.5 us
  transfers between devices with their start and end apart: 1, of which 1 were waited for; matrix products, arithmetic and copies ran while one was open for 0% of the time, Pallas kernels for 0%

commit v1 on v0

--- a/solution.py
+++ b/solution.py
@@ -105,15 +105,104 @@
     return jnp.concatenate(rows, axis=0)
 
 
+def group_width(count, peers):
+    groups = peers // 2
+    return -(-count // (groups * TILE)) * TILE
+
+
+class Sum:
+    def __init__(self, peers, factor, grads, part, pair, mid, got, full, send, recv):
+        self.peers, self.factor = peers, factor
+        self.grads, self.part, self.pair, self.mid, self.got, self.full = grads, part, pair, mid, got, full
+        self.send, self.recv = send, recv
+        self.me, self.rep = lax.axis_index("space"), lax.axis_index("rep")
+        self.groups = peers // 2
+        self.width = part.shape[2]
+
+    def copy(self, src, dst, n, chip, core):
+        return pltpu.make_async_remote_copy(
+            src_ref=src, dst_ref=dst, send_sem=self.send.at[n], recv_sem=self.recv.at[n],
+            device_id=(chip, core), device_id_type=MESH,
+        )
+
+    def pair_copy(self):
+        other = 1 - self.rep
+        src = self.part.at[pl.ds(other * self.peers, self.peers)]
+        return self.copy(src, self.pair, 0, self.me, other)
+
+    def share_copy(self, o):
+        chip = lax.rem(self.me + o, self.peers)
+        return self.copy(self.mid.at[chip], self.got.at[o], o, chip, self.rep)
+
+    def total_copy(self, o, owner):
+        chip = lax.rem(self.me + o, self.peers)
+        spot = self.full.at[self.rep * self.peers + owner]
+        return self.copy(spot, spot, self.peers + o, chip, self.rep)
+
+    def core_copy(self, o):
+        owner = lax.rem(self.me + self.peers - o, self.peers)
+        spot = self.full.at[self.rep * self.peers + owner]
+        return self.copy(spot, spot, 2 * self.peers + o, self.me, 1 - self.rep)
+
+    def each(self, start, act):
+        lax.fori_loop(start, self.peers, lambda o, c: (act(o), c)[1], 0)
+
+    def begin(self):
+        w = self.width
+        for row in range(4):
+            for col in range(self.groups):
+                self.part[row * self.groups + col] = self.grads[
+                    16 * row : 16 * row + 16, col * w : (col + 1) * w
+                ].astype(BF16)
+        self.pair_copy().start()
+
+    def scatter(self):
+        self.pair_copy().wait()
+        mine = self.part[pl.ds(self.rep * self.peers, self.peers)]
+        self.mid[...] = (mine.astype(F32) + self.pair[...].astype(F32)).astype(BF16)
+        self.each(1, lambda o: self.share_copy(o).start())
+
+    def gather(self):
+        self.each(1, lambda o: self.share_copy(o).wait())
+        total = self.mid[self.me].astype(F32)
+        for o in range(1, self.peers):
+            total = total + self.got[o].astype(F32)
+        self.full[self.rep * self.peers + self.me] = (total * self.factor).astype(BF16)
+        self.core_copy(0).start()
+        self.each(1, lambda o: self.total_copy(o, self.me).start())
+
+    def finish(self, out):
+        def pass_on(o):
+            owner = lax.rem(self.me + self.peers - o, self.peers)
+            self.total_copy(o, owner).wait_recv()
+            self.core_copy(o).start()
+
+        self.each(1, pass_on)
+        self.each(1, lambda o: self.total_copy(o, self.me).wait_send())
+        self.each(0, lambda o: self.core_copy(o).wait())
+        w = self.width
+        for row in range(4):
+            for col in range(self.groups):
+                end = min((col + 1) * w, out.shape[1])
+                if end > col * w:
+                    out[16 * row : 16 * row + 16, col * w : end] = self.full[
+                        row * self.groups + col, :, : end - col * w
+                    ].astype(F32)
+
+
 def body(
-    peers,
+    peers, factor,
     f_ref, nb_ref, sl_ref, cot_ref, wf_ref, wd_ref, wc_ref, wct_ref, wu_ref, wdt_ref, wut_ref,
     e0_ref, q0_ref, q2_ref, pm_ref,
-    out_ref, grads_ref,
+    out_ref, second_ref, first_ref,
     x0, fh, fl, sl_lo, sl_hi, sm_lo, sm_hi, idx, r0, slope0, p2, c2, h1, h1_lo, h1_hi,
     cand, r1, rim, rim_lo, rim_hi, dg0, dgm, dgp, gh1, gh0,
     send_sem, recv_sem, local_sem,
+    *sums,
 ):
+    second_sum = Sum(peers, factor, *sums[:8])
+    first_sum = Sum(peers, factor, *sums[8:])
+    second_grads, first_grads = second_sum.grads, first_sum.grads
     nb, ch = f_ref.shape[0], f_ref.shape[1]
     cells = HALF**3
     me = lax.axis_index("space")
@@ -122,9 +211,15 @@
     down = lax.rem(me + peers - 1, peers)
 
     barrier = pltpu.get_barrier_semaphore()
-    for other in (up, down):
+
+    def greet(o, carry):
+        other = lax.rem(me + o, peers)
         pl.semaphore_signal(barrier, inc=1, device_id=(other, rep), device_id_type=MESH)
-    pl.semaphore_wait(barrier, 2)
+        return carry
+
+    lax.fori_loop(1, peers, greet, 0)
+    pl.semaphore_signal(barrier, inc=1, device_id=(me, 1 - rep), device_id_type=MESH)
+    pl.semaphore_wait(barrier, peers)
 
     def remote(src, dst, n, other):
         copy = pltpu.make_async_remote_copy(
@@ -327,14 +422,19 @@
     taps = 9 * ch
     grad_coarse = sum(dot_t(placed(delta_up[p], HALF), r1[p]) for p in range(pairs))
     for a in range(3):
-        grads_ref[:, (3 + a) * taps : (4 + a) * taps] = grad_coarse[a * ch : (a + 1) * ch]
-    grads_ref[:, 6 * taps + 8 * ch : 6 * taps + 16 * ch] = dot_t(gated, c2[...])
+        second_grads[:, a * taps : (a + 1) * taps] = grad_coarse[a * ch : (a + 1) * ch]
+    held = 3 * taps + 8 * ch
+    second_grads[:, 3 * taps : held] = dot_t(gated, c2[...])
+    for ref in (first_grads, second_grads):
+        ref[:, held:] = jnp.zeros((ch, ref.shape[1] - held), F32)
+    second_sum.begin()
 
     dg0[nb] = jnp.zeros(dg0.shape[1:], F32)
     dgm[none] = jnp.zeros(dg0.shape[1:], F32)
     dgp[none] = jnp.zeros(dg0.shape[1:], F32)
     for copy in third:
         copy.wait()
+    second_sum.scatter()
     for p in range(pairs):
         for h in range(2):
             x = turn(rim_hi[p].astype(F32), -h * cells).astype(BF16)
@@ -350,7 +450,7 @@
             sums[chunk % 2] = sums[chunk % 2] + table[idx[b, k], :, t * TILE : (t + 1) * TILE]
         gh1[:, b * cells : (b + 1) * cells] = sums[0][:, :cells] + sums[1][:, cells:]
     delta_down = (gh1[...] * slope_down).astype(BF16)
-    grads_ref[:, 6 * taps : 6 * taps + 8 * ch] = dot_t(delta_down, p2[...])
+    first_grads[:, 3 * taps : held] = dot_t(delta_down, p2[...])
     gh0[...] = c2[...].astype(F32) + dot(wdt_ref[...], delta_down)
     grad_fine = jnp.zeros((3 * ch, taps), F32)
     for b in range(nb):
@@ -359,7 +459,13 @@
         delta = (wide_grad * slope0[b]).astype(BF16)
         grad_fine = grad_fine + dot_t(placed(delta, EDGE), r0[b])
     for a in range(3):
-        grads_ref[:, a * taps : (a + 1) * taps] = grad_fine[a * ch : (a + 1) * ch]
+        first_grads[:, a * taps : (a + 1) * taps] = grad_fine[a * ch : (a + 1) * ch]
+    first_sum.begin()
+    second_sum.gather()
+    first_sum.scatter()
+    second_sum.finish(second_ref)
+    first_sum.gather()
+    first_sum.finish(first_ref)
 
 
 def shards(features, neighbours, send_list, w_fine, w_down, w_coarse, w_up, cotangent):
@@ -377,14 +483,28 @@
     smem = pl.BlockSpec(memory_space=pltpu.SMEM)
     v = pltpu.VMEM
     width = 10 * HALF**3
-    decoded, grads = pl.pallas_call(
-        functools.partial(body, peers),
+    factor = 1.0 / math.sqrt(lax.axis_size("rep") * peers * nb * EDGE**3)
+    count = 3 * taps + 8 * ch
+    share = group_width(count, peers)
+    sums = [
+        v((ch, peers // 2 * share), F32),
+        v((2 * peers, 16, share), BF16),
+        v((peers, 16, share), BF16),
+        v((peers, 16, share), BF16),
+        v((peers, 16, share), BF16),
+        v((2 * peers, 16, share), BF16),
+        pltpu.SemaphoreType.DMA((3 * peers,)),
+        pltpu.SemaphoreType.DMA((3 * peers,)),
+    ]
+    decoded, second, first = pl.pallas_call(
+        functools.partial(body, peers, factor),
         out_shape=(
             jax.ShapeDtypeStruct(features.shape[1:], BF16),
-            jax.ShapeDtypeStruct((ch, 6 * taps + 16 * ch), F32),
+            jax.ShapeDtypeStruct((ch, count), F32),
+            jax.ShapeDtypeStruct((ch, count), F32),
         ),
         in_specs=[vmem, smem] + [vmem] * 13,
-        out_specs=(vmem, vmem),
+        out_specs=(vmem, vmem, vmem),
         scratch_shapes=[
             v((nb + 1, ch, EDGE**3), BF16),
             v((2 * nb + 1, ch, TILE), BF16),
@@ -414,6 +534,8 @@
             pltpu.SemaphoreType.DMA((8,)),
             pltpu.SemaphoreType.DMA((8,)),
             pltpu.SemaphoreType.DMA((2,)),
+            *sums,
+            *sums,
         ],
         compiler_params=pltpu.CompilerParams(
             collective_id=0, has_side_effects=True, vmem_limit_bytes=56 * 1024 * 1024
@@ -422,10 +544,8 @@
         features[0], neighbours[0], send_list[0, 0], cotangent[0],
         stacked(w_fine), w_down, stacked(w_coarse), wct, w_up, w_down.T, w_up.T, *consts,
     )
-    factor = 1.0 / math.sqrt(lax.axis_size("rep") * peers * nb * EDGE**3)
-    grads = lax.psum(grads, ("space", "rep")) * factor
-    a, b, c = 3 * taps, 6 * taps, 6 * taps + 8 * ch
-    return decoded[None], grads[:, :a], grads[:, b:c], grads[:, a:b], grads[:, c:]
+    cut = 3 * taps
+    return decoded[None], first[:, :cut], first[:, cut:], second[:, :cut], second[:, cut:]
 
 
 def solution(mesh):

time: 196 us -> 71.1 us (0.36)
  waiting for transfers between devices: 132 us -> 0 us
  Pallas kernels: 38.5 us -> 57.9 us
  between operations: 14.1 us -> 0.7 us
  local copies, waits for them, and re-layouts: 9.49 us -> 12.2 us
    psum x1 -> x0, waiting for transfers between devices: 132 us -> none  [shards(): grads = lax.psum(grads, ('space', 'rep')) * factor]
    pallas_call x1, Pallas kernels: 38.5 us -> 57.9 us  [shards(): pl.pallas_call(functools.partial(body, peers, factor), out_shape=(jax.Sha...]
    slice x2 -> x4, local copies, waits for them, and re-layouts: 1.77 us -> 5.1 us  [the longest x1 1.81 us: shards(): first[:, :cut]]
  transfers between devices with their start and end apart: 1 -> 0, of which waited for: 1 -> 0; matrix products, arithmetic and copies ran while one was open for 0% -> 0% of each run, Pallas kernels for 0% -> 0%
where the time goes in v1:
time: 71.1 us; the launch traced here: 70.9 us
  Pallas kernels  57.9 us (81%)
  local copies, waits for them, and re-layouts  12.2 us (17%)
    pallas_call x1, Pallas kernels, shards(): pl.pallas_call(functools.partial(body, peers, factor), out_shape=(jax.Sha...  57.9 us
    unnamed x14, local copies, waits for them, and re-layouts  3.91 us
    slice x1, local copies, waits for them, and re-layouts, shards(): first[:, :cut]  1.81 us
    slice x1, local copies, waits for them, and re-layouts, shards(): first[:, cut:]  1.73 us
    transpose x2, local copies, waits for them, and re-layouts, stacked(): return w.reshape(ch, 3, taps).transpose(1, 0, 2).reshape(3 * ch, taps)  1.44 us
    reshape x2, local copies, waits for them, and re-layouts, shards(): w_coarse.reshape(ch, 3, 9, ch).transpose(1, 3, 2, 0).reshape(3 * ch, taps)  1.43 us

profile of v1, /device:TPU:0, one launch (start us, length us, event | category | flops | bytes accessed | tf_op | source)
XLA Modules:
  0.0 70.9 jit_solution(16706069115835193441)
XLA Ops:
  0.6 0.0 copy-start.2
  0.6 0.0 copy-start.4
  0.7 1.6 %copy.26 = bf16[64,512]{0,1:T(8,128)(2,1)} copy(bf16[64,512]{1,0:T(8,128)(2,1)} %wd_ref.1) | data formatting | bytes 131072 | tf_op args[4]
  2.3 0.0 copy-done.2
  2.3 0.8 %copy.27 = bf16[64,512]{0,1:T(8,128)(2,1)} copy(bf16[64,512]{1,0:T(8,128)(2,1)S(1)} %copy-done.2) | data formatting | bytes 131072 | tf_op args[6]
  3.1 0.0 copy-done.4
  3.1 0.2 reshape.28
  3.2 0.0 copy-start
  3.3 0.7 %copy.22 = bf16[3,64,576]{2,1,0:T(8,128)(2,1)} copy(bf16[3,64,576]{2,0,1:T(4,128)(2,1)S(1)} %bitcast.15) | data formatting | bytes 442368 | tf_op jit(solution)/shard_map/transpose | solution.py:478
  4.0 0.3 copy-done
  4.3 0.2 reshape.30
  4.5 0.7 %copy.23 = bf16[3,64,576]{2,1,0:T(8,128)(2,1)} copy(bf16[3,64,576]{2,0,1:T(4,128)(2,1)S(1)} %bitcast.16) | data formatting | bytes 442368 | tf_op jit(solution)/shard_map/transpose | solution.py:478
  5.2 0.3 copy.24
  5.5 0.3 copy.29
  5.8 1.1 %reshape.34.wct_ref = bf16[192,576]{1,0:T(8,128)(2,1)} reshape(bf16[3,64,9,64]{3,2,1,0:T(8,128)(2,1)S(1)} %copy.29) | data formatting | bytes 442368 | tf_op jit(solution)/shard_map/reshape | solution.py:480
  6.9 57.9 %shard_map.155 = (bf16[4,64,512]{2,1,0:T(8,128)(2,1)}, f32[64,2240]{1,0:T(8,128)}, f32[64,2240]{1,0:T(8,128)}) custom-call(bf16[4,64,512]{2,1,0:T(8,128)(2,1)} %bitcast.21, s32[4,26]{1,0:T(4,128)} %bitcast.24, s32[2,16]{1,0:T(2,128)} %bitcast.25, bf16[4,64,512]{2,1,0:T(8,128)(2,1)} %bitcast.22, bf16[192,576]{1,0:T(8,128)(2,1)} %bitcast.17, ...), custom_call_target="tpu_custom_call" | custom-call | tf_op jit(solution)/shard_map/pallas_call | solution.py:499
  64.8 0.0 copy-start.1
  64.8 1.7 %slice.13 = f32[64,512]{1,0:T(8,128)} slice(f32[64,2240]{1,0:T(8,128)} %get-tuple-element.9), slice={[0:64], [1728:2240]} | slice | bytes 262144 | tf_op jit(solution)/shard_map/slice | solution.py:548
  66.6 1.8 %slice.12 = f32[64,1728]{1,0:T(8,128)} slice(f32[64,2240]{1,0:T(8,128)} %get-tuple-element.9), slice={[0:64], [0:1728]} | slice | bytes 884736 | tf_op jit(solution)/shard_map/slice | solution.py:548
  68.4 0.0 copy-done.1
  68.4 0.8 %slice.15 = f32[64,512]{1,0:T(8,128)} slice(f32[64,2240]{1,0:T(8,128)S(1)} %copy-done.1), slice={[0:64], [1728:2240]} | slice | bytes 262144 | tf_op jit(solution)/shard_map/slice | solution.py:548
  69.1 0.0 copy-start.3
  69.1 0.8 %slice.14 = f32[64,1728]{1,0:T(8,128)} slice(f32[64,2240]{1,0:T(8,128)S(1)} %copy-done.1), slice={[0:64], [0:1728]} | slice | bytes 884736 | tf_op jit(solution)/shard_map/slice | solution.py:548
  69.9 0.2 copy-done.3
  70.2 0.7 copy.32
Async XLA Ops:
  0.6 1.7 %copy-start.2 = (bf16[64,512]{1,0:T(8,128)(2,1)S(1)}, bf16[64,512]{1,0:T(8,128)(2,1)}, u32[]{:S(2)}) copy-start(bf16[64,512]{1,0:T(8,128)(2,1)} %wu_ref.1) | copy-start | bytes 196612
  0.6 2.4 %copy-start.4 = (bf16[64,1728]{1,0:T(8,128)(2,1)S(1)}, bf16[64,1728]{1,0:T(8,128)(2,1)}, u32[]{:S(2)}) copy-start(bf16[64,1728]{1,0:T(8,128)(2,1)} %param.15) | copy-start | bytes 663556
  3.2 1.0 %copy-start = (bf16[64,1728]{1,0:T(8,128)(2,1)S(1)}, bf16[64,1728]{1,0:T(8,128)(2,1)}, u32[]{:S(2)}) copy-start(bf16[64,1728]{1,0:T(8,128)(2,1)} %param.17) | copy-start | bytes 663556
  64.8 3.6 %copy-start.1 = (f32[64,2240]{1,0:T(8,128)S(1)}, f32[64,2240]{1,0:T(8,128)}, u32[]{:S(2)}) copy-start(f32[64,2240]{1,0:T(8,128)} %get-tuple-element.10) | copy-start | bytes 1720324
  69.1 1.0 %copy-start.3 = (bf16[4,64,512]{2,1,0:T(8,128)(2,1)S(1)}, bf16[4,64,512]{2,1,0:T(8,128)(2,1)}, u32[]{:S(2)}) copy-start(bf16[4,64,512]{2,1,0:T(8,128)(2,1)} %get-tuple-element.8) | copy-start | bytes 786436

commit v2 on v1

--- a/solution.py
+++ b/solution.py
@@ -171,7 +171,7 @@
         self.core_copy(0).start()
         self.each(1, lambda o: self.total_copy(o, self.me).start())
 
-    def finish(self, out):
+    def finish(self, outs):
         def pass_on(o):
             owner = lax.rem(self.me + self.peers - o, self.peers)
             self.total_copy(o, owner).wait_recv()
@@ -180,21 +180,25 @@
         self.each(1, pass_on)
         self.each(1, lambda o: self.total_copy(o, self.me).wait_send())
         self.each(0, lambda o: self.core_copy(o).wait())
-        w = self.width
-        for row in range(4):
-            for col in range(self.groups):
-                end = min((col + 1) * w, out.shape[1])
-                if end > col * w:
-                    out[16 * row : 16 * row + 16, col * w : end] = self.full[
-                        row * self.groups + col, :, : end - col * w
+        per = self.width // TILE
+        tile = 0
+        for out in outs:
+            for start in range(0, out.shape[1], TILE):
+                size = min(TILE, out.shape[1] - start)
+                inner = tile % per * TILE
+                for row in range(4):
+                    out[16 * row : 16 * row + 16, start : start + size] = self.full[
+                        row * self.groups + tile // per, :, inner : inner + size
                     ].astype(F32)
+                tile += 1
 
 
 def body(
     peers, factor,
-    f_ref, nb_ref, sl_ref, cot_ref, wf_ref, wd_ref, wc_ref, wct_ref, wu_ref, wdt_ref, wut_ref,
+    f_ref, nb_ref, sl_ref, cot_ref, w_fine, wd_ref, w_coarse, wu_ref,
     e0_ref, q0_ref, q2_ref, pm_ref,
-    out_ref, second_ref, first_ref,
+    out_ref, grad_fine_ref, grad_down_ref, grad_coarse_ref, grad_up_ref,
+    wf_ref, wc_ref, wct_ref, a0,
     x0, fh, fl, sl_lo, sl_hi, sm_lo, sm_hi, idx, r0, slope0, p2, c2, h1, h1_lo, h1_hi,
     cand, r1, rim, rim_lo, rim_hi, dg0, dgm, dgp, gh1, gh0,
     send_sem, recv_sem, local_sem,
@@ -244,15 +248,30 @@
     fh[2 * nb] = jnp.zeros(fh.shape[1:], BF16)
     fl[2 * nb] = jnp.zeros(fl.shape[1:], BF16)
 
-    def to_patches(src, dst, b):
+    def to_patches(src, dst):
         moved = dot(src, pm_ref[...]).astype(BF16)
-        for part in range(8):
-            dst[part * ch : (part + 1) * ch, b * cells : (b + 1) * cells] = moved[
-                :, part * cells : (part + 1) * cells
-            ]
-
-    for b in range(nb):
-        to_patches(cot_ref[b], c2, b)
+        for b in range(nb):
+            for part in range(8):
+                dst[part * ch : (part + 1) * ch, b * cells : (b + 1) * cells] = moved[
+                    b * ch : (b + 1) * ch, part * cells : (part + 1) * cells
+                ]
+
+    def by_block(value):
+        return [value[b * ch : (b + 1) * ch] for b in range(nb)]
+
+    taps = 9 * ch
+    for a in range(3):
+        wf_ref[a * ch : (a + 1) * ch, :] = w_fine[:, a * taps : (a + 1) * taps]
+        wc_ref[a * ch : (a + 1) * ch, :] = w_coarse[:, a * taps : (a + 1) * taps]
+    for n in range(0, 27, 2):
+        size = min(2, 27 - n)
+        flipped = w_coarse[:, n * ch : (n + size) * ch].astype(F32).T.astype(BF16)
+        for m in range(size):
+            a, k = (n + m) // 9, (n + m) % 9
+            wct_ref[a * ch : (a + 1) * ch, k * ch : (k + 1) * ch] = flipped[m * ch : (m + 1) * ch]
+    wdt = wd_ref[...].astype(F32).T.astype(BF16)
+    wut = wu_ref[...].astype(F32).T.astype(BF16)
+    to_patches(jnp.concatenate([cot_ref[b] for b in range(nb)], axis=0), c2)
 
     first[0].wait()
     first[1].wait()
@@ -287,33 +306,53 @@
     e0 = e0_ref[...]
     e0c = e0_ref[4 * TILE : 5 * TILE, :]
     for b in range(nb):
-        rows = []
-        for t in range(4):
-            rows.append(
-                jnp.concatenate(
-                    [x0[idx[b, 9 + n], :, t * TILE : (t + 1) * TILE] for n in range(9)], axis=1
-                )
-            )
-        inner = dot(jnp.concatenate(rows, axis=0), e0)
-        low = dot(jnp.concatenate([fh[idx[b, n]] for n in range(9)], axis=1), e0[:, TILE:])
-        high = dot(jnp.concatenate([fl[idx[b, 18 + n]] for n in range(9)], axis=1), e0[:, :TILE])
-        pad = jnp.concatenate(
-            [low] + [inner[t * ch : (t + 1) * ch] for t in range(4)] + [high], axis=1
+        for n in range(9):
+            for t in range(4):
+                row = (4 * b + t) * ch
+                a0[row : row + ch, n * TILE : (n + 1) * TILE] = x0[
+                    idx[b, 9 + n], :, t * TILE : (t + 1) * TILE
+                ]
+    inner = dot(a0[...], e0)
+
+    def faces(table, i):
+        return jnp.concatenate(
+            [
+                jnp.concatenate([table[idx[b, 9 * i + n]] for n in range(9)], axis=1)
+                for b in range(nb)
+            ],
+            axis=0,
         )
+
+    low = by_block(dot(faces(fh, 0), e0[:, TILE:]))
+    high = by_block(dot(faces(fl, 2), e0[:, :TILE]))
+    wide = EDGE * TILE
+    hidden0 = []
+    for b in range(nb):
+        middle = [inner[(4 * b + t) * ch : (4 * b + t + 1) * ch] for t in range(4)]
+        pad = jnp.concatenate([low[b]] + middle + [high[b]], axis=1)
         for n in range(9):
             off = (EDGE + 2) * (n // 3 - 1) + n % 3 - 1
             r0[b, n * ch : (n + 1) * ch, :] = turn(pad, -off).astype(BF16)
         y = dot(wf_ref[...], r0[b])
-        wide = EDGE * TILE
         v = sum(y[a * ch : (a + 1) * ch, a * TILE : a * TILE + wide] for a in range(3))
         s = sigmoid(v)
         slope0[b] = s * (1.0 + v * (1.0 - s))
         h = (v * s).astype(BF16)
-        flat = jnp.concatenate(
-            [dot_t(h[:, 2 * TILE * t : 2 * TILE * (t + 1)], e0c).astype(BF16) for t in range(4)],
-            axis=1,
+        hidden0 += [h[:, 2 * TILE * t : 2 * TILE * (t + 1)] for t in range(4)]
+    flat = dot_t(jnp.concatenate(hidden0, axis=0), e0c).astype(BF16)
+
+    def rows_to_lanes(value):
+        return jnp.concatenate(
+            [
+                jnp.concatenate(
+                    [value[(4 * b + t) * ch : (4 * b + t + 1) * ch] for t in range(4)], axis=1
+                )
+                for b in range(nb)
+            ],
+            axis=0,
         )
-        to_patches(flat, p2, b)
+
+    to_patches(rows_to_lanes(flat), p2)
 
     coarse_pre = dot(wd_ref[...], p2[...])
     s = sigmoid(coarse_pre)
@@ -350,50 +389,50 @@
     q0 = q0_ref[...]
     top = (HALF - 1) * TILE
 
-    def sources(b, i):
-        parts = []
-        for t in range(5):
-            x = cand[i, 0, idx[b, 9 * i + 2 * t]]
-            if t < 4:
-                x = x + cand[i, 1, idx[b, 9 * i + 2 * t + 1]]
-            parts.append(x)
-        return jnp.concatenate(parts, axis=1)
+    def sources(i):
+        rows = []
+        for b in range(nb):
+            parts = []
+            for t in range(5):
+                x = cand[i, 0, idx[b, 9 * i + 2 * t]]
+                if t < 4:
+                    x = x + cand[i, 1, idx[b, 9 * i + 2 * t + 1]]
+                parts.append(x)
+            rows.append(jnp.concatenate(parts, axis=1))
+        return jnp.concatenate(rows, axis=0)
 
     pairs = nb // 2
     wide1 = HALF * TILE
-    gated = []
-    delta_up = []
+    pads = by_block(
+        jnp.concatenate(
+            [dot(sources(0), q0[:, top:]), dot(sources(1), q0), dot(sources(2), q0[:, :TILE])],
+            axis=1,
+        )
+    )
+    pre, ups = [], []
     for p in range(pairs):
-        pads = []
-        for b in (2 * p, 2 * p + 1):
-            pads.append(
-                jnp.concatenate(
-                    [
-                        dot(sources(b, 0), q0[:, top:]),
-                        dot(sources(b, 1), q0),
-                        dot(sources(b, 2), q0[:, :TILE]),
-                    ],
-                    axis=1,
-                )
-            )
-        pad = pads[0] + turn(pads[1], cells)
+        pad = pads[2 * p] + turn(pads[2 * p + 1], cells)
         for n in range(9):
             off = (HALF + 2) * (n // 3 - 1) + n % 3 - 1
             r1[p, n * ch : (n + 1) * ch, :] = turn(pad, -off).astype(BF16)
         y = dot(wc_ref[...], r1[p])
-        v = sum(y[a * ch : (a + 1) * ch, a * TILE : a * TILE + wide1] for a in range(3))
-        s = sigmoid(v)
-        slope = s * (1.0 + v * (1.0 - s))
-        gated.append(dot_t((v * s).astype(BF16), q2_ref[...]).astype(BF16))
-        ub = split_dot(dot, up_back[:, p * TILE : (p + 1) * TILE], q2_ref[...])
-        delta = (ub * slope).astype(BF16)
-        delta_up.append(delta)
+        pre.append(sum(y[a * ch : (a + 1) * ch, a * TILE : a * TILE + wide1] for a in range(3)))
+        ups.append(up_back[:, p * TILE : (p + 1) * TILE])
+    v = jnp.concatenate(pre, axis=0)
+    s = sigmoid(v)
+    slope = s * (1.0 + v * (1.0 - s))
+    gated = dot_t((v * s).astype(BF16), q2_ref[...]).astype(BF16)
+    delta = (split_dot(dot, jnp.concatenate(ups, axis=0), q2_ref[...]) * slope).astype(BF16)
+    delta_up = [delta[p * ch : (p + 1) * ch] for p in range(pairs)]
+    gated = jnp.concatenate([gated[p * ch : (p + 1) * ch] for p in range(pairs)], axis=1)
+    gap = jnp.zeros((ch, TILE), F32)
+    backs = []
+    for p in range(pairs):
         turned = []
         for n in range(9):
             off = (HALF + 2) * (n // 3 - 1) + n % 3 - 1
-            turned.append(turn(delta.astype(F32), off).astype(BF16))
+            turned.append(turn(delta_up[p].astype(F32), off).astype(BF16))
         y = dot(wct_ref[...], jnp.concatenate(turned, axis=0))
-        gap = jnp.zeros((ch, TILE), F32)
         back = (
             jnp.concatenate([y[:ch], gap, gap], axis=1)
             + jnp.concatenate([gap, y[ch : 2 * ch], gap], axis=1)
@@ -401,46 +440,59 @@
         )
         rim[0, p] = back[:, :TILE].astype(BF16)
         rim[1, p] = back[:, -TILE:].astype(BF16)
-        for h in range(2):
-            b = 2 * p + h
-            x = turn(back, -h * cells)
-            dg0[b] = split_dot(dot_t, x[:, TILE : TILE + wide1], q0)
-            dgm[b] = split_dot(dot_t, x[:, :TILE], q0[:, top:])
-            dgp[b] = split_dot(dot_t, x[:, -TILE:], q0[:, :TILE])
+        backs += [back, turn(back, -cells)]
     third = [remote(rim.at[0], rim_hi, 6, down), remote(rim.at[1], rim_lo, 7, up)]
 
-    gated = jnp.concatenate(gated, axis=1)
-    dec = (p2[...].astype(F32) + dot(wut_ref[...], gated)).astype(BF16)
-
-    def from_patches(value, b):
+    backs = jnp.concatenate(backs, axis=0)
+    for table, value, spread in (
+        (dg0, backs[:, TILE : TILE + wide1], q0),
+        (dgm, backs[:, :TILE], q0[:, top:]),
+        (dgp, backs[:, -TILE:], q0[:, :TILE]),
+    ):
+        for b, x in enumerate(by_block(split_dot(dot_t, value, spread))):
+            table[b] = x
+
+    dec = (p2[...].astype(F32) + dot(wut, gated)).astype(BF16)
+
+    def from_patches(value):
         return jnp.concatenate(
-            [value[n * ch : (n + 1) * ch, b * cells : (b + 1) * cells] for n in range(8)], axis=1
+            [
+                jnp.concatenate(
+                    [
+                        value[n * ch : (n + 1) * ch, b * cells : (b + 1) * cells]
+                        for n in range(8)
+                    ],
+                    axis=1,
+                )
+                for b in range(nb)
+            ],
+            axis=0,
         )
 
-    for b in range(nb):
-        out_ref[b] = dot_t(from_patches(dec, b), pm_ref[...]).astype(BF16)
-    taps = 9 * ch
+    for b, x in enumerate(by_block(dot_t(from_patches(dec), pm_ref[...]).astype(BF16))):
+        out_ref[b] = x
+    held = 8 * ch
+    second_grads[:, :held] = dot_t(gated, c2[...])
     grad_coarse = sum(dot_t(placed(delta_up[p], HALF), r1[p]) for p in range(pairs))
     for a in range(3):
-        second_grads[:, a * taps : (a + 1) * taps] = grad_coarse[a * ch : (a + 1) * ch]
-    held = 3 * taps + 8 * ch
-    second_grads[:, 3 * taps : held] = dot_t(gated, c2[...])
-    for ref in (first_grads, second_grads):
-        ref[:, held:] = jnp.zeros((ch, ref.shape[1] - held), F32)
-    second_sum.begin()
+        start = 2 * held + a * taps
+        second_grads[:, start : start + taps] = grad_coarse[a * ch : (a + 1) * ch]
+    for ref, used in ((first_grads, 3 * taps), (second_grads, 3 * taps + 2 * held)):
+        ref[:, used:] = jnp.zeros((ch, ref.shape[1] - used), F32)
 
     dg0[nb] = jnp.zeros(dg0.shape[1:], F32)
     dgm[none] = jnp.zeros(dg0.shape[1:], F32)
     dgp[none] = jnp.zeros(dg0.shape[1:], F32)
     for copy in third:
         copy.wait()
-    second_sum.scatter()
-    for p in range(pairs):
-        for h in range(2):
-            x = turn(rim_hi[p].astype(F32), -h * cells).astype(BF16)
-            dgm[nb + 2 * p + h] = dot_t(x, q0[:, top:])
-            x = turn(rim_lo[p].astype(F32), -h * cells).astype(BF16)
-            dgp[nb + 2 * p + h] = dot_t(x, q0[:, :TILE])
+    for table, ref, spread in ((dgm, rim_hi, q0[:, top:]), (dgp, rim_lo, q0[:, :TILE])):
+        rows = []
+        for p in range(pairs):
+            x = ref[p].astype(F32)
+            rows += [x, turn(x, -cells)]
+        rows = jnp.concatenate(rows, axis=0).astype(BF16)
+        for b, x in enumerate(by_block(dot_t(rows, spread))):
+            table[nb + b] = x
     for b in range(nb):
         sums = [nothing, nothing]
         for k in range(27):
@@ -450,22 +502,29 @@
             sums[chunk % 2] = sums[chunk % 2] + table[idx[b, k], :, t * TILE : (t + 1) * TILE]
         gh1[:, b * cells : (b + 1) * cells] = sums[0][:, :cells] + sums[1][:, cells:]
     delta_down = (gh1[...] * slope_down).astype(BF16)
-    first_grads[:, 3 * taps : held] = dot_t(delta_down, p2[...])
-    gh0[...] = c2[...].astype(F32) + dot(wdt_ref[...], delta_down)
+    second_grads[:, held : 2 * held] = dot_t(delta_down, p2[...])
+    second_sum.begin()
+    gh0[...] = c2[...].astype(F32) + dot(wdt, delta_down)
+    flat = dot_t(from_patches(gh0[...]).astype(BF16), pm_ref[...]).astype(BF16)
+    spread = jnp.concatenate(
+        [flat[b * ch : (b + 1) * ch, t * TILE : (t + 1) * TILE] for b in range(nb) for t in range(4)],
+        axis=0,
+    )
+    wide_grad = by_block(rows_to_lanes(dot(spread, e0c)))
+    second_sum.scatter()
     grad_fine = jnp.zeros((3 * ch, taps), F32)
     for b in range(nb):
-        flat = dot_t(from_patches(gh0[...], b).astype(BF16), pm_ref[...]).astype(BF16)
-        wide_grad = jnp.concatenate([dot(t, e0c) for t in tiles(flat)], axis=1)
-        delta = (wide_grad * slope0[b]).astype(BF16)
+        delta = (wide_grad[b] * slope0[b]).astype(BF16)
         grad_fine = grad_fine + dot_t(placed(delta, EDGE), r0[b])
+        if b == nb // 2:
+            second_sum.gather()
     for a in range(3):
         first_grads[:, a * taps : (a + 1) * taps] = grad_fine[a * ch : (a + 1) * ch]
     first_sum.begin()
-    second_sum.gather()
     first_sum.scatter()
-    second_sum.finish(second_ref)
+    second_sum.finish([grad_up_ref, grad_down_ref, grad_coarse_ref])
     first_sum.gather()
-    first_sum.finish(first_ref)
+    first_sum.finish([grad_fine_ref])
 
 
 def shards(features, neighbours, send_list, w_fine, w_down, w_coarse, w_up, cotangent):
@@ -474,38 +533,39 @@
     peers = lax.axis_size("space")
     taps = 9 * ch
 
-    def stacked(w):
-        return w.reshape(ch, 3, taps).transpose(1, 0, 2).reshape(3 * ch, taps)
-
-    wct = w_coarse.reshape(ch, 3, 9, ch).transpose(1, 3, 2, 0).reshape(3 * ch, taps)
     consts = [jnp.asarray(t(), BF16) for t in (fine_spread, coarse_spread, pair_spread, patch_order)]
     vmem = pl.BlockSpec(memory_space=pltpu.VMEM)
     smem = pl.BlockSpec(memory_space=pltpu.SMEM)
     v = pltpu.VMEM
     width = 10 * HALF**3
     factor = 1.0 / math.sqrt(lax.axis_size("rep") * peers * nb * EDGE**3)
-    count = 3 * taps + 8 * ch
-    share = group_width(count, peers)
-    sums = [
-        v((ch, peers // 2 * share), F32),
-        v((2 * peers, 16, share), BF16),
-        v((peers, 16, share), BF16),
-        v((peers, 16, share), BF16),
-        v((peers, 16, share), BF16),
-        v((2 * peers, 16, share), BF16),
-        pltpu.SemaphoreType.DMA((3 * peers,)),
-        pltpu.SemaphoreType.DMA((3 * peers,)),
-    ]
-    decoded, second, first = pl.pallas_call(
+
+    def sum_buffers(count):
+        share = group_width(count, peers)
+        return [
+            v((ch, peers // 2 * share), F32),
+            v((2 * peers, 16, share), BF16),
+            v((peers, 16, share), BF16),
+            v((peers, 16, share), BF16),
+            v((peers, 16, share), BF16),
+            v((2 * peers, 16, share), BF16),
+            pltpu.SemaphoreType.DMA((3 * peers,)),
+            pltpu.SemaphoreType.DMA((3 * peers,)),
+        ]
+
+    decoded, *grads = pl.pallas_call(
         functools.partial(body, peers, factor),
         out_shape=(
             jax.ShapeDtypeStruct(features.shape[1:], BF16),
-            jax.ShapeDtypeStruct((ch, count), F32),
-            jax.ShapeDtypeStruct((ch, count), F32),
+            *[jax.ShapeDtypeStruct(w.shape, F32) for w in (w_fine, w_down, w_coarse, w_up)],
         ),
-        in_specs=[vmem, smem] + [vmem] * 13,
-        out_specs=(vmem, vmem, vmem),
+        in_specs=[vmem, smem] + [vmem] * 10,
+        out_specs=(vmem,) * 5,
         scratch_shapes=[
+            v((3 * ch, taps), BF16),
+            v((3 * ch, taps), BF16),
+            v((3 * ch, taps), BF16),
+            v((4 * nb * ch, 9 * TILE), BF16),
             v((nb + 1, ch, EDGE**3), BF16),
             v((2 * nb + 1, ch, TILE), BF16),
             v((2 * nb + 1, ch, TILE), BF16),
@@ -534,18 +594,17 @@
             pltpu.SemaphoreType.DMA((8,)),
             pltpu.SemaphoreType.DMA((8,)),
             pltpu.SemaphoreType.DMA((2,)),
-            *sums,
-            *sums,
+            *sum_buffers(3 * taps + 16 * ch),
+            *sum_buffers(3 * taps),
         ],
         compiler_params=pltpu.CompilerParams(
             collective_id=0, has_side_effects=True, vmem_limit_bytes=56 * 1024 * 1024
         ),
     )(
         features[0], neighbours[0], send_list[0, 0], cotangent[0],
-        stacked(w_fine), w_down, stacked(w_coarse), wct, w_up, w_down.T, w_up.T, *consts,
+        w_fine, w_down, w_coarse, w_up, *consts,
     )
-    cut = 3 * taps
-    return decoded[None], first[:, :cut], first[:, cut:], second[:, :cut], second[:, cut:]
+    return decoded[None], *grads
 
 
 def solution(mesh):

time: 71.1 us -> 61.6 us (0.87)
  local copies, waits for them, and re-layouts: 12.2 us -> 5.06 us
  Pallas kernels: 57.9 us -> 55.6 us
    slice x4 -> x0, local copies, waits for them, and re-layouts: 5.1 us -> none  [the longest x1 1.81 us: shards(): first[:, :cut]]
    pallas_call x1, Pallas kernels: 57.9 us -> 55.6 us  [shards(): pl.pallas_call(functools.partial(body, peers, factor), out_shape=(jax.Sha...]
    reshape x4 -> x0, local copies, waits for them, and re-layouts: 1.79 us -> none  [the longest x2 1.43 us: shards(): w_coarse.reshape(ch, 3, 9, ch).transpose(1, 3, 2, 0).reshape(3 * ch, taps)]
    transpose x2 -> x0, local copies, waits for them, and re-layouts: 1.44 us -> none  [stacked(): return w.reshape(ch, 3, taps).transpose(1, 0, 2).reshape(3 * ch, taps)]
    unnamed x14 -> x13, local copies, waits for them, and re-layouts: 3.91 us -> 5.06 us
where the time goes in v2:
time: 61.6 us; the launch traced here: 61.3 us
  Pallas kernels  55.6 us (90%)
  local copies, waits for them, and re-layouts  5.06 us (8%)
  between operations  0.66 us (1%)
    pallas_call x1, Pallas kernels, shards(): pl.pallas_call(functools.partial(body, peers, factor), out_shape=(jax.Sha...  55.6 us
    unnamed x13, local copies, waits for them, and re-layouts  5.06 us

profile of v2, /device:TPU:0, one launch (start us, length us, event | category | flops | bytes accessed | tf_op | source)
XLA Modules:
  0.0 61.3 jit_solution(5147439268374700850)
XLA Ops:
  0.6 55.6 %shard_map.155 = (bf16[4,64,512]{2,1,0:T(8,128)(2,1)}, f32[64,1728]{1,0:T(8,128)}, f32[64,512]{1,0:T(8,128)}, f32[64,1728]{1,0:T(8,128)}, f32[64,512]{1,0:T(8,128)}) custom-call(bf16[4,64,512]{2,1,0:T(8,128)(2,1)} %bitcast.5, s32[4,26]{1,0:T(4,128)} %bitcast.8, s32[2,16]{1,0:T(2,128)} %bitcast.9, bf16[4,64,512]{2,1,0:T(8,128)(2,1)} %bitcast.6, ...), custom_call_target="tpu_custom_call" | custom-call | tf_op jit(solution)/shard_map/pallas_call | solution.py:556
  56.3 0.0 copy-start.1
  56.3 1.7 %copy.22 = bf16[1,4,64,512]{3,2,1,0:T(8,128)(2,1)} copy(bf16[1,4,64,512]{3,2,1,0:T(8,128)(2,1)} %bitcast.7) | data formatting | bytes 524288
  58.0 0.0 copy-done.1
  58.0 0.0 copy-start.3
  58.0 0.0 copy-start
  58.0 0.8 %copy.23 = f32[64,1728]{1,0:T(8,128)} copy(f32[64,1728]{1,0:T(8,128)S(1)} %copy-done.1) | data formatting | bytes 884736
  58.8 0.2 copy-done.3
  59.0 0.7 %copy.24 = f32[64,512]{1,0:T(8,128)} copy(f32[64,512]{1,0:T(8,128)S(1)} %copy-done.3) | data formatting | bytes 262144
  59.7 0.0 copy-done
  59.7 0.0 copy-start.2
  59.7 0.8 %copy.25 = f32[64,1728]{1,0:T(8,128)} copy(f32[64,1728]{1,0:T(8,128)S(1)} %copy-done) | data formatting | bytes 884736
  60.4 0.3 copy-done.2
  60.7 0.7 %copy.26 = f32[64,512]{1,0:T(8,128)} copy(f32[64,512]{1,0:T(8,128)S(1)} %copy-done.2) | data formatting | bytes 262144
Async XLA Ops:
  56.3 1.7 %copy-start.1 = (f32[64,1728]{1,0:T(8,128)S(1)}, f32[64,1728]{1,0:T(8,128)}, u32[]{:S(2)}) copy-start(f32[64,1728]{1,0:T(8,128)} %get-tuple-element.21) | copy-start | bytes 1327108
  58.0 1.0 %copy-start.3 = (f32[64,512]{1,0:T(8,128)S(1)}, f32[64,512]{1,0:T(8,128)}, u32[]{:S(2)}) copy-start(f32[64,512]{1,0:T(8,128)} %get-tuple-element.22) | copy-start | bytes 393220
  58.0 1.7 %copy-start = (f32[64,1728]{1,0:T(8,128)S(1)}, f32[64,1728]{1,0:T(8,128)}, u32[]{:S(2)}) copy-start(f32[64,1728]{1,0:T(8,128)} %get-tuple-element.23) | copy-start | bytes 1327108
  59.7 1.0 %copy-start.2 = (f32[64,512]{1,0:T(8,128)S(1)}, f32[64,512]{1,0:T(8,128)}, u32[]{:S(2)}) copy-start(f32[64,512]{1,0:T(8,128)} %get-tuple-element.24) | copy-start | bytes 393220

commit v3 on v2

--- a/solution.py
+++ b/solution.py
@@ -92,17 +92,23 @@
     return 1.0 / (1.0 + jnp.exp(-v))
 
 
-def placed(x, tile_count):
-    rows = []
+def placed_rows(x):
+    columns = []
     for a in range(3):
         parts = []
         if a:
-            parts.append(jnp.zeros((x.shape[0], a * TILE), x.dtype))
+            parts.append(jnp.zeros((a * TILE, x.shape[1]), x.dtype))
         parts.append(x)
         if a < 2:
-            parts.append(jnp.zeros((x.shape[0], (2 - a) * TILE), x.dtype))
-        rows.append(jnp.concatenate(parts, axis=1))
-    return jnp.concatenate(rows, axis=0)
+            parts.append(jnp.zeros(((2 - a) * TILE, x.shape[1]), x.dtype))
+        columns.append(jnp.concatenate(parts, axis=0))
+    return jnp.concatenate(columns, axis=1)
+
+
+def flipped(x):
+    return jnp.concatenate(
+        [x[:, t : min(t + TILE, x.shape[1])].T for t in range(0, x.shape[1], TILE)], axis=0
+    )
 
 
 def group_width(count, peers):
@@ -171,7 +177,7 @@
         self.core_copy(0).start()
         self.each(1, lambda o: self.total_copy(o, self.me).start())
 
-    def finish(self, outs):
+    def finish(self, out):
         def pass_on(o):
             owner = lax.rem(self.me + self.peers - o, self.peers)
             self.total_copy(o, owner).wait_recv()
@@ -180,24 +186,32 @@
         self.each(1, pass_on)
         self.each(1, lambda o: self.total_copy(o, self.me).wait_send())
         self.each(0, lambda o: self.core_copy(o).wait())
-        per = self.width // TILE
+        out[...] = self.full[...]
+
+
+def unpack(groups, dec_in, second, first, dec_out, fine, down, coarse, up, sem):
+    copy = pltpu.make_async_copy(dec_in, dec_out, sem)
+    copy.start()
+    for full, outs in ((second, (up, down, coarse)), (first, (fine,))):
+        per = full.shape[2] // TILE
         tile = 0
         for out in outs:
             for start in range(0, out.shape[1], TILE):
                 size = min(TILE, out.shape[1] - start)
                 inner = tile % per * TILE
                 for row in range(4):
-                    out[16 * row : 16 * row + 16, start : start + size] = self.full[
-                        row * self.groups + tile // per, :, inner : inner + size
+                    out[16 * row : 16 * row + 16, start : start + size] = full[
+                        row * groups + tile // per, :, inner : inner + size
                     ].astype(F32)
                 tile += 1
+    copy.wait()
 
 
 def body(
     peers, factor,
     f_ref, nb_ref, sl_ref, cot_ref, w_fine, wd_ref, w_coarse, wu_ref,
     e0_ref, q0_ref, q2_ref, pm_ref,
-    out_ref, grad_fine_ref, grad_down_ref, grad_coarse_ref, grad_up_ref,
+    out_ref, second_ref, first_ref,
     wf_ref, wc_ref, wct_ref, a0,
     x0, fh, fl, sl_lo, sl_hi, sm_lo, sm_hi, idx, r0, slope0, p2, c2, h1, h1_lo, h1_hi,
     cand, r1, rim, rim_lo, rim_hi, dg0, dgm, dgp, gh1, gh0,
@@ -265,10 +279,10 @@
         wc_ref[a * ch : (a + 1) * ch, :] = w_coarse[:, a * taps : (a + 1) * taps]
     for n in range(0, 27, 2):
         size = min(2, 27 - n)
-        flipped = w_coarse[:, n * ch : (n + size) * ch].astype(F32).T.astype(BF16)
+        turned = w_coarse[:, n * ch : (n + size) * ch].astype(F32).T.astype(BF16)
         for m in range(size):
             a, k = (n + m) // 9, (n + m) % 9
-            wct_ref[a * ch : (a + 1) * ch, k * ch : (k + 1) * ch] = flipped[m * ch : (m + 1) * ch]
+            wct_ref[a * ch : (a + 1) * ch, k * ch : (k + 1) * ch] = turned[m * ch : (m + 1) * ch]
     wdt = wd_ref[...].astype(F32).T.astype(BF16)
     wut = wu_ref[...].astype(F32).T.astype(BF16)
     to_patches(jnp.concatenate([cot_ref[b] for b in range(nb)], axis=0), c2)
@@ -326,14 +340,15 @@
     low = by_block(dot(faces(fh, 0), e0[:, TILE:]))
     high = by_block(dot(faces(fl, 2), e0[:, :TILE]))
     wide = EDGE * TILE
+    span = wide + 2 * TILE
     hidden0 = []
     for b in range(nb):
         middle = [inner[(4 * b + t) * ch : (4 * b + t + 1) * ch] for t in range(4)]
         pad = jnp.concatenate([low[b]] + middle + [high[b]], axis=1)
         for n in range(9):
             off = (EDGE + 2) * (n // 3 - 1) + n % 3 - 1
-            r0[b, n * ch : (n + 1) * ch, :] = turn(pad, -off).astype(BF16)
-        y = dot(wf_ref[...], r0[b])
+            r0[n * ch : (n + 1) * ch, b * span : (b + 1) * span] = turn(pad, -off).astype(BF16)
+        y = dot(wf_ref[...], r0[:, b * span : (b + 1) * span])
         v = sum(y[a * ch : (a + 1) * ch, a * TILE : a * TILE + wide] for a in range(3))
         s = sigmoid(v)
         slope0[b] = s * (1.0 + v * (1.0 - s))
@@ -381,11 +396,6 @@
                 for n in range(nb, 2 * nb):
                     cand[table, half, n] = nothing.astype(BF16)
     up_back = dot(wu_ref[...], c2[...])
-    for copy in second:
-        copy.wait()
-    candidates(h1_lo[...], 0, nb)
-    candidates(h1_hi[...], 2, nb)
-
     q0 = q0_ref[...]
     top = (HALF - 1) * TILE
 
@@ -403,9 +413,15 @@
 
     pairs = nb // 2
     wide1 = HALF * TILE
+    inner1 = dot(sources(1), q0)
+    for copy in second:
+        copy.wait()
+    candidates(h1_lo[...], 0, nb)
+    candidates(h1_hi[...], 2, nb)
+
     pads = by_block(
         jnp.concatenate(
-            [dot(sources(0), q0[:, top:]), dot(sources(1), q0), dot(sources(2), q0[:, :TILE])],
+            [dot(sources(0), q0[:, top:]), inner1, dot(sources(2), q0[:, :TILE])],
             axis=1,
         )
     )
@@ -449,7 +465,7 @@
         (dgm, backs[:, :TILE], q0[:, top:]),
         (dgp, backs[:, -TILE:], q0[:, :TILE]),
     ):
-        for b, x in enumerate(by_block(split_dot(dot_t, value, spread))):
+        for b, x in enumerate(by_block(dot_t(value.astype(BF16), spread))):
             table[b] = x
 
     dec = (p2[...].astype(F32) + dot(wut, gated)).astype(BF16)
@@ -473,7 +489,9 @@
         out_ref[b] = x
     held = 8 * ch
     second_grads[:, :held] = dot_t(gated, c2[...])
-    grad_coarse = sum(dot_t(placed(delta_up[p], HALF), r1[p]) for p in range(pairs))
+    grad_coarse = flipped(
+        sum(dot(r1[p], placed_rows(delta_up[p].astype(F32).T.astype(BF16))) for p in range(pairs))
+    )
     for a in range(3):
         start = 2 * held + a * taps
         second_grads[:, start : start + taps] = grad_coarse[a * ch : (a + 1) * ch]
@@ -512,19 +530,22 @@
     )
     wide_grad = by_block(rows_to_lanes(dot(spread, e0c)))
     second_sum.scatter()
-    grad_fine = jnp.zeros((3 * ch, taps), F32)
-    for b in range(nb):
-        delta = (wide_grad[b] * slope0[b]).astype(BF16)
-        grad_fine = grad_fine + dot_t(placed(delta, EDGE), r0[b])
-        if b == nb // 2:
+    grad_fine = []
+    for half in range(2):
+        blocks = range(half * nb // 2, (half + 1) * nb // 2)
+        deltas = [placed_rows((wide_grad[b] * slope0[b]).T.astype(BF16)) for b in blocks]
+        cols = r0[:, blocks.start * span : blocks.stop * span]
+        grad_fine.append(dot(cols, jnp.concatenate(deltas, axis=0)))
+        if half == 0:
             second_sum.gather()
+    grad_fine = flipped(grad_fine[0] + grad_fine[1])
     for a in range(3):
         first_grads[:, a * taps : (a + 1) * taps] = grad_fine[a * ch : (a + 1) * ch]
     first_sum.begin()
     first_sum.scatter()
-    second_sum.finish([grad_up_ref, grad_down_ref, grad_coarse_ref])
+    second_sum.finish(second_ref)
     first_sum.gather()
-    first_sum.finish([grad_fine_ref])
+    first_sum.finish(first_ref)
 
 
 def shards(features, neighbours, send_list, w_fine, w_down, w_coarse, w_up, cotangent):
@@ -540,8 +561,7 @@
     width = 10 * HALF**3
     factor = 1.0 / math.sqrt(lax.axis_size("rep") * peers * nb * EDGE**3)
 
-    def sum_buffers(count):
-        share = group_width(count, peers)
+    def sum_buffers(share):
         return [
             v((ch, peers // 2 * share), F32),
             v((2 * peers, 16, share), BF16),
@@ -553,14 +573,15 @@
             pltpu.SemaphoreType.DMA((3 * peers,)),
         ]
 
-    decoded, *grads = pl.pallas_call(
+    shares = [group_width(n, peers) for n in (3 * taps + 16 * ch, 3 * taps)]
+    half_done = pl.pallas_call(
         functools.partial(body, peers, factor),
         out_shape=(
             jax.ShapeDtypeStruct(features.shape[1:], BF16),
-            *[jax.ShapeDtypeStruct(w.shape, F32) for w in (w_fine, w_down, w_coarse, w_up)],
+            *[jax.ShapeDtypeStruct((2 * peers, 16, share), BF16) for share in shares],
         ),
         in_specs=[vmem, smem] + [vmem] * 10,
-        out_specs=(vmem,) * 5,
+        out_specs=(vmem,) * 3,
         scratch_shapes=[
             v((3 * ch, taps), BF16),
             v((3 * ch, taps), BF16),
@@ -574,7 +595,7 @@
             pltpu.SMEM(send_list.shape[2:], jnp.int32),
             pltpu.SMEM(send_list.shape[2:], jnp.int32),
             pltpu.SMEM((nb, 27), jnp.int32),
-            v((nb, taps, (EDGE + 2) * TILE), BF16),
+            v((taps, nb * (EDGE + 2) * TILE), BF16),
             v((nb, ch, EDGE * TILE), F32),
             v((8 * ch, cols), BF16),
             v((8 * ch, cols), BF16),
@@ -594,8 +615,8 @@
             pltpu.SemaphoreType.DMA((8,)),
             pltpu.SemaphoreType.DMA((8,)),
             pltpu.SemaphoreType.DMA((2,)),
-            *sum_buffers(3 * taps + 16 * ch),
-            *sum_buffers(3 * taps),
+            *sum_buffers(shares[0]),
+            *sum_buffers(shares[1]),
         ],
         compiler_params=pltpu.CompilerParams(
             collective_id=0, has_side_effects=True, vmem_limit_bytes=56 * 1024 * 1024
@@ -604,6 +625,18 @@
         features[0], neighbours[0], send_list[0, 0], cotangent[0],
         w_fine, w_down, w_coarse, w_up, *consts,
     )
+    anywhere = pl.BlockSpec(memory_space=pl.ANY)
+    decoded, *grads = pl.pallas_call(
+        functools.partial(unpack, peers // 2),
+        out_shape=(
+            jax.ShapeDtypeStruct(features.shape[1:], BF16),
+            *[jax.ShapeDtypeStruct(w.shape, F32) for w in (w_fine, w_down, w_coarse, w_up)],
+        ),
+        in_specs=[anywhere, vmem, vmem],
+        out_specs=(anywhere, vmem, vmem, vmem, vmem),
+        scratch_shapes=[pltpu.SemaphoreType.DMA],
+        compiler_params=pltpu.CompilerParams(vmem_limit_bytes=32 * 1024 * 1024),
+    )(*half_done)
     return decoded[None], *grads
 
 

time: 61.6 us -> 63.2 us (1.026)
  Pallas kernels: 55.6 us -> 59.2 us
  local copies, waits for them, and re-layouts: 5.06 us -> 2.89 us
    unnamed x13 -> x6, local copies, waits for them, and re-layouts: 5.06 us -> 2.89 us
    pallas_call x1, Pallas kernels: 55.6 us -> 57.5 us  [shards(): pl.pallas_call(functools.partial(body, peers, factor), out_shape=(jax.Sha...]
    pallas_call x0 -> x1, Pallas kernels: none -> 1.71 us  [shards(): pl.pallas_call(functools.partial(unpack, peers // 2), out_shape=(jax.Shap...]
where the time goes in v3:
time: 63.2 us; the launch traced here: 62.9 us
  Pallas kernels  59.2 us (94%)
  local copies, waits for them, and re-layouts  2.89 us (5%)
  between operations  0.81 us (1%)
    pallas_call x1, Pallas kernels, shards(): pl.pallas_call(functools.partial(body, peers, factor), out_shape=(jax.Sha...  57.5 us
    unnamed x6, local copies, waits for them, and re-layouts  2.89 us
    pallas_call x1, Pallas kernels, shards(): pl.pallas_call(functools.partial(unpack, peers // 2), out_shape=(jax.Shap...  1.71 us

profile of v3, /device:TPU:0, one launch (start us, length us, event | category | flops | bytes accessed | tf_op | source)
XLA Modules:
  0.0 62.9 jit_solution(14887929304770803002)
XLA Ops:
  0.6 57.5 %shard_map.155 = (bf16[4,64,512]{2,1,0:T(8,128)(2,1)}, bf16[32,16,384]{2,1,0:T(8,128)(2,1)}, bf16[32,16,256]{2,1,0:T(8,128)(2,1)}) custom-call(bf16[4,64,512]{2,1,0:T(8,128)(2,1)} %bitcast.5, s32[4,26]{1,0:T(4,128)} %bitcast.7, s32[2,16]{1,0:T(2,128)} %bitcast.8, bf16[4,64,512]{2,1,0:T(8,128)(2,1)} %bitcast.6, bf16[64,1728]{1,0:T(8,128)(2,1)} %w_fine.1, ...), custom_call_target="tpu_custom_call" | custom-call | tf_op jit(solution)/shard_map/pallas_call | solution.py:577
  58.2 0.0 copy-start
  58.2 1.0 %copy-done = bf16[32,16,384]{2,1,0:T(8,128)(2,1)S(1)} copy-done((bf16[32,16,384]{2,1,0:T(8,128)(2,1)S(1)}, bf16[32,16,384]{2,1,0:T(8,128)(2,1)}, u32[]{:S(2)}) %copy-start) | copy-done | bytes 393240
  59.2 0.0 copy-start.1
  59.2 0.9 %copy-done.1 = bf16[4,64,512]{2,1,0:T(8,128)(2,1)S(1)} copy-done((bf16[4,64,512]{2,1,0:T(8,128)(2,1)S(1)}, bf16[4,64,512]{2,1,0:T(8,128)(2,1)}, u32[]{:S(2)}) %copy-start.1) | copy-done | bytes 262168
  60.1 0.0 copy-start.2
  60.1 0.9 %copy-done.2 = bf16[32,16,256]{2,1,0:T(8,128)(2,1)S(1)} copy-done((bf16[32,16,256]{2,1,0:T(8,128)(2,1)S(1)}, bf16[32,16,256]{2,1,0:T(8,128)(2,1)}, u32[]{:S(2)}) %copy-start.2) | copy-done | bytes 262168
  61.1 1.7 %shard_map.156 = (bf16[4,64,512]{2,1,0:T(8,128)(2,1)}, f32[64,1728]{1,0:T(8,128)}, f32[64,512]{1,0:T(8,128)}, f32[64,1728]{1,0:T(8,128)}, f32[64,512]{1,0:T(8,128)}) custom-call(bf16[4,64,512]{2,1,0:T(8,128)(2,1)S(1)} %copy-done.1, bf16[32,16,384]{2,1,0:T(8,128)(2,1)S(1)} %copy-done, bf16[32,16,256]{2,1,0:T(8,128)(2,1)S(1)} %copy-done.2), custom_call_target="tpu_custom_call" | custom-call | tf_op jit(solution)/shard_map/pallas_call | solution.py:629
Async XLA Ops:
  58.2 1.0 %copy-start = (bf16[32,16,384]{2,1,0:T(8,128)(2,1)S(1)}, bf16[32,16,384]{2,1,0:T(8,128)(2,1)}, u32[]{:S(2)}) copy-start(bf16[32,16,384]{2,1,0:T(8,128)(2,1)} %get-tuple-element.14.second) | copy-start | bytes 1179652
  59.2 0.9 %copy-start.1 = (bf16[4,64,512]{2,1,0:T(8,128)(2,1)S(1)}, bf16[4,64,512]{2,1,0:T(8,128)(2,1)}, u32[]{:S(2)}) copy-start(bf16[4,64,512]{2,1,0:T(8,128)(2,1)} %get-tuple-element.13.dec_in) | copy-start | bytes 786436
  60.1 0.9 %copy-start.2 = (bf16[32,16,256]{2,1,0:T(8,128)(2,1)S(1)}, bf16[32,16,256]{2,1,0:T(8,128)(2,1)}, u32[]{:S(2)}) copy-start(bf16[32,16,256]{2,1,0:T(8,128)(2,1)} %get-tuple-element.15.first) | copy-start | bytes 786436

commit v4 on v3

--- a/solution.py
+++ b/solution.py
@@ -92,23 +92,17 @@
     return 1.0 / (1.0 + jnp.exp(-v))
 
 
-def placed_rows(x):
-    columns = []
+def placed(x, tile_count):
+    rows = []
     for a in range(3):
         parts = []
         if a:
-            parts.append(jnp.zeros((a * TILE, x.shape[1]), x.dtype))
+            parts.append(jnp.zeros((x.shape[0], a * TILE), x.dtype))
         parts.append(x)
         if a < 2:
-            parts.append(jnp.zeros(((2 - a) * TILE, x.shape[1]), x.dtype))
-        columns.append(jnp.concatenate(parts, axis=0))
-    return jnp.concatenate(columns, axis=1)
-
-
-def flipped(x):
-    return jnp.concatenate(
-        [x[:, t : min(t + TILE, x.shape[1])].T for t in range(0, x.shape[1], TILE)], axis=0
-    )
+            parts.append(jnp.zeros((x.shape[0], (2 - a) * TILE), x.dtype))
+        rows.append(jnp.concatenate(parts, axis=1))
+    return jnp.concatenate(rows, axis=0)
 
 
 def group_width(count, peers):
@@ -177,13 +171,15 @@
         self.core_copy(0).start()
         self.each(1, lambda o: self.total_copy(o, self.me).start())
 
-    def finish(self, out):
+    def forward(self):
         def pass_on(o):
             owner = lax.rem(self.me + self.peers - o, self.peers)
             self.total_copy(o, owner).wait_recv()
             self.core_copy(o).start()
 
         self.each(1, pass_on)
+
+    def finish(self, out):
         self.each(1, lambda o: self.total_copy(o, self.me).wait_send())
         self.each(0, lambda o: self.core_copy(o).wait())
         out[...] = self.full[...]
@@ -273,6 +269,43 @@
     def by_block(value):
         return [value[b * ch : (b + 1) * ch] for b in range(nb)]
 
+    none = 2 * nb
+    for b in range(nb):
+        for k in range(9, 18):
+            v = jnp.int32(b) if k == 13 else nb_ref[b, k if k < 13 else k - 1]
+            idx[b, k] = jnp.where(v < 0, nb, v)
+
+    e0 = e0_ref[...]
+    e0c = e0_ref[4 * TILE : 5 * TILE, :]
+    for b in range(nb):
+        for n in range(9):
+            for t in range(4):
+                row = (4 * b + t) * ch
+                a0[row : row + ch, n * TILE : (n + 1) * TILE] = x0[
+                    idx[b, 9 + n], :, t * TILE : (t + 1) * TILE
+                ]
+    inner = dot(a0[...], e0)
+
+    first[0].wait()
+    first[1].wait()
+    to_smem = [
+        pltpu.make_async_copy(sl_lo, sm_lo, local_sem.at[0]),
+        pltpu.make_async_copy(sl_hi, sm_hi, local_sem.at[1]),
+    ]
+    for copy in to_smem:
+        copy.start()
+    for copy in to_smem:
+        copy.wait()
+    slots = sl_ref.shape[1]
+    for b in range(nb):
+        for k in range(9):
+            v = nb_ref[b, k]
+            far = nb + sm_lo[0, jnp.clip(v - nb, 0, slots - 1)]
+            idx[b, k] = jnp.where(v < 0, none, jnp.where(v < nb, v, far))
+        for k in range(18, 27):
+            v = nb_ref[b, k - 1]
+            far = nb + sm_hi[1, jnp.clip(v - nb - slots, 0, slots - 1)]
+            idx[b, k] = jnp.where(v < 0, none, jnp.where(v < nb, v, far))
     taps = 9 * ch
     for a in range(3):
         wf_ref[a * ch : (a + 1) * ch, :] = w_fine[:, a * taps : (a + 1) * taps]
@@ -287,46 +320,8 @@
     wut = wu_ref[...].astype(F32).T.astype(BF16)
     to_patches(jnp.concatenate([cot_ref[b] for b in range(nb)], axis=0), c2)
 
-    first[0].wait()
-    first[1].wait()
-    to_smem = [
-        pltpu.make_async_copy(sl_lo, sm_lo, local_sem.at[0]),
-        pltpu.make_async_copy(sl_hi, sm_hi, local_sem.at[1]),
-    ]
-    for copy in to_smem:
-        copy.start()
-    for copy in to_smem:
-        copy.wait()
-    slots = sl_ref.shape[1]
-    none = 2 * nb
-    for b in range(nb):
-        for k in range(27):
-            if k == 13:
-                idx[b, k] = jnp.int32(b)
-                continue
-            v = nb_ref[b, k if k < 13 else k - 1]
-            if k < 9:
-                far = nb + sm_lo[0, jnp.clip(v - nb, 0, slots - 1)]
-                v = jnp.where(v < 0, none, jnp.where(v < nb, v, far))
-            elif k >= 18:
-                far = nb + sm_hi[1, jnp.clip(v - nb - slots, 0, slots - 1)]
-                v = jnp.where(v < 0, none, jnp.where(v < nb, v, far))
-            else:
-                v = jnp.where(v < 0, nb, v)
-            idx[b, k] = v
     first[2].wait()
     first[3].wait()
-
-    e0 = e0_ref[...]
-    e0c = e0_ref[4 * TILE : 5 * TILE, :]
-    for b in range(nb):
-        for n in range(9):
-            for t in range(4):
-                row = (4 * b + t) * ch
-                a0[row : row + ch, n * TILE : (n + 1) * TILE] = x0[
-                    idx[b, 9 + n], :, t * TILE : (t + 1) * TILE
-                ]
-    inner = dot(a0[...], e0)
 
     def faces(table, i):
         return jnp.concatenate(
@@ -489,9 +484,7 @@
         out_ref[b] = x
     held = 8 * ch
     second_grads[:, :held] = dot_t(gated, c2[...])
-    grad_coarse = flipped(
-        sum(dot(r1[p], placed_rows(delta_up[p].astype(F32).T.astype(BF16))) for p in range(pairs))
-    )
+    grad_coarse = sum(dot_t(placed(delta_up[p], HALF), r1[p]) for p in range(pairs))
     for a in range(3):
         start = 2 * held + a * taps
         second_grads[:, start : start + taps] = grad_coarse[a * ch : (a + 1) * ch]
@@ -530,21 +523,20 @@
     )
     wide_grad = by_block(rows_to_lanes(dot(spread, e0c)))
     second_sum.scatter()
-    grad_fine = []
-    for half in range(2):
-        blocks = range(half * nb // 2, (half + 1) * nb // 2)
-        deltas = [placed_rows((wide_grad[b] * slope0[b]).T.astype(BF16)) for b in blocks]
-        cols = r0[:, blocks.start * span : blocks.stop * span]
-        grad_fine.append(dot(cols, jnp.concatenate(deltas, axis=0)))
-        if half == 0:
+    grad_fine = jnp.zeros((3 * ch, taps), F32)
+    for b in range(nb):
+        delta = (wide_grad[b] * slope0[b]).astype(BF16)
+        grad_fine = grad_fine + dot_t(placed(delta, EDGE), r0[:, b * span : (b + 1) * span])
+        if b == nb // 2:
             second_sum.gather()
-    grad_fine = flipped(grad_fine[0] + grad_fine[1])
     for a in range(3):
         first_grads[:, a * taps : (a + 1) * taps] = grad_fine[a * ch : (a + 1) * ch]
     first_sum.begin()
     first_sum.scatter()
+    second_sum.forward()
+    first_sum.gather()
     second_sum.finish(second_ref)
-    first_sum.gather()
+    first_sum.forward()
     first_sum.finish(first_ref)
 
 
@@ -635,7 +627,7 @@
         in_specs=[anywhere, vmem, vmem],
         out_specs=(anywhere, vmem, vmem, vmem, vmem),
         scratch_shapes=[pltpu.SemaphoreType.DMA],
-        compiler_params=pltpu.CompilerParams(vmem_limit_bytes=32 * 1024 * 1024),
+        compiler_params=pltpu.CompilerParams(vmem_limit_bytes=60 * 1024 * 1024),
     )(*half_done)
     return decoded[None], *grads
 

time: 63.2 us -> 66 us (1.044)
  Pallas kernels: 59.2 us -> 65.2 us
  local copies, waits for them, and re-layouts: 2.89 us -> 0 us
    pallas_call x1, Pallas kernels: 1.71 us -> 11.1 us  [shards(): pl.pallas_call(functools.partial(unpack, peers // 2), out_shape=(jax.Shap...]
    pallas_call x1, Pallas kernels: 57.5 us -> 54.1 us  [shards(): pl.pallas_call(functools.partial(body, peers, factor), out_shape=(jax.Sha...]
    unnamed x6 -> x0, local copies, waits for them, and re-layouts: 2.89 us -> none
where the time goes in v4:
time: 66 us; the launch traced here: 65.8 us
  Pallas kernels  65.2 us (99%)
    pallas_call x1, Pallas kernels, shards(): pl.pallas_call(functools.partial(body, peers, factor), out_shape=(jax.Sha...  54.1 us
    pallas_call x1, Pallas kernels, shards(): pl.pallas_call(functools.partial(unpack, peers // 2), out_shape=(jax.Shap...  11.1 us

profile of v4, /device:TPU:0, one launch (start us, length us, event | category | flops | bytes accessed | tf_op | source)
XLA Modules:
  0.0 65.8 jit_solution(18324162796559997013)
XLA Ops:
  0.6 54.1 %shard_map.155 = (bf16[4,64,512]{2,1,0:T(8,128)(2,1)}, bf16[32,16,384]{2,1,0:T(8,128)(2,1)}, bf16[32,16,256]{2,1,0:T(8,128)(2,1)}) custom-call(bf16[4,64,512]{2,1,0:T(8,128)(2,1)} %bitcast.5, s32[4,26]{1,0:T(4,128)} %bitcast.7, s32[2,16]{1,0:T(2,128)} %bitcast.8, bf16[4,64,512]{2,1,0:T(8,128)(2,1)} %bitcast.6, bf16[64,1728]{1,0:T(8,128)(2,1)} %w_fine.1, ...), custom_call_target="tpu_custom_call" | custom-call | tf_op jit(solution)/shard_map/pallas_call | solution.py:569
  54.7 11.1 %shard_map.156 = (bf16[4,64,512]{2,1,0:T(8,128)(2,1)}, f32[64,1728]{1,0:T(8,128)}, f32[64,512]{1,0:T(8,128)}, f32[64,1728]{1,0:T(8,128)}, f32[64,512]{1,0:T(8,128)}) custom-call(bf16[4,64,512]{2,1,0:T(8,128)(2,1)} %get-tuple-element.13.dec_in, bf16[32,16,384]{2,1,0:T(8,128)(2,1)} %get-tuple-element.14.second, bf16[32,16,256]{2,1,0:T(8,128)(2,1)} %get-tuple-element.15.first), custom_call_target="tpu_custom_call" | custom-call | tf_op jit(solution)/shard_map/pallas_call | solution.py:621
